TPU v7x, 32 devices: a whole 2x2x4 slice. The times are simulated.
32 devices in a mesh: grp: 2 (over y), chan: 4 (over x, core), freq: 4 (over z).
Axes of the slice: x: 2, y: 2, z: 4, core: 2. Of those that a mesh axis runs over, the one named last changes fastest.
Arguments:
- phases: float32 [32, 2048, 256], P(('grp', 'freq'), 'chan'), parts along dimension 0, may hold values from -3.140625 to 3.140625
- tile_pairs: int32 [4, 2, 2], P('chan'), may hold values from 0 to 3
- block_offsets: int32 [4, 2], P('chan'), may hold values from 0 to 1, each once within a row
- owners: int32 [4, 2, 1], P('chan'), may hold values from 0 to 3; in each aligned block of 2 rows (0 to 1, 2 to 3, ..., all dimensions but the last counted through in order) at most 2 rows name the same one
Outputs:
- envelopes: float32 [64, 32, 16384], P(('grp', 'chan', 'freq')), parts along dimension 0
There are 2 independent parts, one for each index of `grp`. A program takes and returns all parts, laid end to end along the dimension named above; an argument that names none is the same for every part. Nothing has to cross between parts.
Inputs may be any that keep to these rules, and one draw needn't show every extreme that they name: `block_offsets`: each channel block's 2 entries name every value once. `owners`: among the 2 entries of one channel block, no owner is named more than 2 times, and some block names one owner exactly 2 times.
All inputs are finite; a program needn't handle non-finite values.
Results may differ from a plain program's by a relative error of at most 0.0033.
Values may be sent and summed in bfloat16 or wider, within the bound.
A program may use at most 128 MiB of HBM per device.

v0:
```python
import math

import jax
import jax.numpy as jnp
from jax import lax
from jax.sharding import PartitionSpec as P

F = 16
NFFT = 512
TILE = 128
CAP = 2
LAGS = 32


def from_behind(x, axis, by):
    count = lax.axis_size(axis)
    return lax.ppermute(x, axis, [(i, (i + by) % count) for i in range(count)])


def spectra_of(phases):
    return jnp.concatenate([jnp.cos(phases), jnp.sin(phases)], axis=-1).astype(jnp.bfloat16)


def lag_table():
    bins = jnp.arange(F, dtype=jnp.float32) + 32.0
    lag_index = jnp.arange(LAGS, dtype=jnp.float32) - float(LAGS // 2)
    angles = 2.0 * math.pi / NFFT * bins[:, None] * lag_index[None, :]
    cosine = jnp.cos(angles)
    sine_part = jnp.sin(angles)
    real_rows = jnp.concatenate([cosine, sine_part], axis=1)
    imag_rows = jnp.concatenate([-sine_part, cosine], axis=1)
    return jnp.stack([real_rows, imag_rows], axis=1)


def slot_entries(owner_row, owner_count):
    list_len = owner_row.shape[0]
    places = jnp.arange(list_len, dtype=jnp.int32)
    same_owner = owner_row[:, None] == owner_row[None, :]
    earlier_mask = places[None, :] < places[:, None]
    earlier = jnp.sum(jnp.where(same_owner & earlier_mask, 1, 0), axis=1).astype(jnp.int32)
    targets = owner_row * CAP + earlier
    slot_ids = jnp.arange(owner_count * CAP, dtype=jnp.int32)
    matched = targets[None, :] == slot_ids[:, None]
    entries = jnp.sum(jnp.where(matched, places[None, :], 0), axis=1)
    filled = jnp.where(jnp.any(matched, axis=1), 1.0, 0.0).astype(jnp.float32)
    return (entries, filled)


def listed_products(left_rows, left_swap, right_rows):
    real_part = jnp.einsum(
        "feik,efjk->efij", left_rows, right_rows, preferred_element_type=jnp.float32
    )
    imag_part = jnp.einsum(
        "feik,efjk->efij", left_swap, right_rows, preferred_element_type=jnp.float32
    )
    return jnp.stack([real_part, imag_part], axis=2)


def on_device(phases, tile_pairs, block_offsets, owners):
    home_block = spectra_of(phases)
    seg_count = phases.shape[2]
    home_swap = jnp.concatenate(
        [home_block[..., seg_count:], -home_block[..., :seg_count]], axis=-1
    )
    freq_local, block_width, both_parts = home_block.shape
    tile_count = block_width // TILE
    loop_size = lax.axis_size("chan")
    half_loop = loop_size // 2
    owner_count = lax.axis_size("freq")
    rows_t = tile_pairs[0, :, 0]
    offsets = block_offsets[0] + 1
    list_len = offsets.shape[0]
    left_tiles = home_block.reshape(freq_local, tile_count, TILE, both_parts)
    swap_tiles = home_swap.reshape(freq_local, tile_count, TILE, both_parts)
    all_pairs, all_offsets = (
        lax.all_gather(tile_pairs, "chan", axis=0, tiled=True),
        lax.all_gather(block_offsets, "chan", axis=0, tiled=True),
    )
    my_place = lax.axis_index("chan")
    arrived = []
    for offset_step in range(half_loop):
        target = (my_place - (offset_step + 1)) % loop_size
        target_offsets = lax.dynamic_index_in_dim(all_offsets, target, 0, keepdims=False)
        target_cols = lax.dynamic_index_in_dim(all_pairs, target, 0, keepdims=False)[:, 1]
        wanted = jnp.sum(jnp.where(target_offsets == offset_step, target_cols, 0))
        outgoing_tile = lax.dynamic_index_in_dim(left_tiles, wanted, 1, keepdims=False)
        arrived.append(from_behind(outgoing_tile, "chan", -(offset_step + 1)))
    arrived_stack = jnp.stack(arrived, axis=0)
    right_rows = jnp.take(arrived_stack, offsets - 1, axis=0)
    cross_tiles = listed_products(left_tiles[:, rows_t], swap_tiles[:, rows_t], right_rows)
    cross_tiles = cross_tiles.reshape(list_len, freq_local * 2, TILE * TILE)
    entries, filled = slot_entries(owners[0, :, 0], owner_count)
    outgoing = jnp.take(cross_tiles, entries, axis=0) * filled[:, None, None]
    outgoing = outgoing.reshape(owner_count, CAP, freq_local * 2, TILE * TILE)
    lag_rows = lag_table().reshape(owner_count, freq_local * 2, 2 * LAGS)
    env_scale = 1.0 / (F * seg_count)
    lagged = jnp.einsum(
        "pkgx,pgl->klx",
        lax.all_to_all(outgoing, "freq", split_axis=0, concat_axis=0, tiled=True),
        lag_rows,
        precision=lax.Precision.HIGHEST,
    )
    return (lagged[:, :LAGS] ** 2 + lagged[:, LAGS:] ** 2) * env_scale


def solution(mesh):
    in_specs = (
        P(("grp", "freq"), "chan", None),
        P("chan", None, None),
        P("chan", None),
        P("chan", None, None),
    )
    out_specs = P(("grp", "chan", "freq"), None, None)
    return jax.shard_map(
        on_device, mesh=mesh, in_specs=in_specs, out_specs=out_specs, check_vma=False
    )
```

profile of v0, /device:TPU:0, one launch (start us, length us, event | category | flops | bytes accessed | tf_op | source)
XLA Modules:
  0.0 171.9 jit_solution(10819930289546500912)
XLA Ops:
  0.0 6.1 %all-gather = s32[4,1,2]{2,1,0:T(1,128)S(1)} all-gather(s32[1,1,2]{2,1,0:T(1,128)} %bitcast.78), channel_id=1, replica_groups=mesh['grp'=2,'chan'=4,'freq'=4] {'chan'}, dimensions={0}, use_global_device_ids=true | all-gather | bytes 40 | tf_op jit(solution)/shard_map/all_gather | solution.py:77
  6.1 5.5 %all_gather.7 = s32[4,2,2]{2,1,0:T(2,128)S(1)} all-gather(s32[1,2,2]{2,1,0:T(2,128)} %param.5), channel_id=1, replica_groups=mesh['grp'=2,'chan'=4,'freq'=4] {'chan'}, dimensions={0}, use_global_device_ids=true | all-gather | bytes 80 | tf_op jit(solution)/shard_map/all_gather | solution.py:76
  11.6 0.2 slice_reduce_fusion
  11.8 0.7 fusion.13
  15.3 8.0 %sine_convert_fusion = bf16[4,512,256]{2,1,0:T(8,128)(2,1)S(1)} fusion(f32[4,512,256]{2,1,0:T(8,128)} %param.4), kind=kLoop, calls=%fused_computation.16 | loop fusion | flops 524288 | bytes 3145728 | tf_op jit(solution)/shard_map/convert.4
  23.3 7.5 %fusion.20 = (bf16[4,512,256]{2,1,0:T(8,128)(2,1)}, bf16[4,512,256]{2,1,0:T(8,128)(2,1)S(1)}) fusion(f32[4,512,256]{2,1,0:T(8,128)S(1)} %copy-done), kind=kLoop, calls=%fused_computation.72 | loop fusion | flops 2097152 | bytes 4194304 | tf_op jit(solution)/shard_map/neg | solution.py:63
  32.2 1.1 fusion.5
  33.2 1.7 collective-permute-start
  34.9 0.3 collective-permute-start.1
  35.2 0.2 fusion.12
  35.4 0.1 select_reduce_fusion
  35.5 0.1 fusion.11
  35.6 0.1 slice_reduce_fusion.2
  35.7 0.1 reduce_sum.42
  35.8 1.5 pad_maximum_fusion
  37.4 2.8 %pad_maximum_fusion.1 = bf16[4,512,512]{2,1,0:T(8,128)(2,1)} fusion(bf16[4,512,256]{2,1,0:T(8,128)(2,1)} %get-tuple-element.7, bf16[4,512,256]{2,1,0:T(8,128)(2,1)S(1)} %sine_convert_fusion), kind=kLoop, calls=%fused_computation.15 | loop fusion | flops 4194304 | bytes 4194304 | tf_op jit(solution)/shard_map/concatenate | solution.py:62
  40.3 1.6 gather_fusion
  41.9 2.3 %gather_fusion.2 = bf16[2,4,128,512]{3,2,1,0:T(8,128)(2,1)S(1)} fusion(bf16[4,4,128,512]{3,2,1,0:T(8,128)(2,1)} %bitcast.74, s32[1024]{0:T(1024)S(1)} %pad_clamp_fusion.2), kind=kCustom, calls=%fused_computation.2 | custom fusion | bytes 2097160 | tf_op jit(solution)/shard_map/gather | solution.py:90
  44.2 3.0 %collective-permute-done = bf16[4,128,512]{2,1,0:T(8,128)(2,1)} collective-permute-done((bf16[4,128,512]{2,1,0:T(8,128)(2,1)}, bf16[4,128,512]{2,1,0:T(8,128)(2,1)}, u32[]{:S(2)}, u32[]{:S(2)}) %collective-permute-start) | collective-permute-done | bytes 524320 | tf_op jit(solution)/shard_map/ppermute | solution.py:17
  47.2 6.4 %collective-permute-done.1 = bf16[4,128,512]{2,1,0:T(8,128)(2,1)} collective-permute-done((bf16[4,128,512]{2,1,0:T(8,128)(2,1)}, bf16[4,128,512]{2,1,0:T(8,128)(2,1)}, u32[]{:S(2)}, u32[]{:S(2)}) %collective-permute-start.1) | collective-permute-done | bytes 524320 | tf_op jit(solution)/shard_map/ppermute | solution.py:17
  53.5 1.3 pad_maximum_fusion.2
  54.8 1.6 gather_fusion.1
  56.4 1.7 %convolution_bitcast_fusion.2 = f32[2,4,1,128,128]{4,3,1,0,2:T(8,128)S(1)} fusion(bf16[2,4,128,512]{3,2,1,0:T(8,128)(2,1)S(1)} %copy-done.2, bf16[2,4,128,512]{3,2,1,0:T(8,128)(2,1)} %gather_fusion.1, pred[2]{0:T(512)(128)(4,1)S(1)} %compare_and_fusion), kind=kOutput, calls=%fused_computation.19 | convolution fusion | flops 134742016 | bytes 2621442 | tf_op jit(solution)/shard_map/feik,efjk->efij/dot_general | solution.py:50
  58.1 1.7 %convolution_bitcast_fusion.1 = f32[2,4,1,128,128]{4,3,1,0,2:T(8,128)S(1)} fusion(bf16[2,4,128,512]{3,2,1,0:T(8,128)(2,1)S(1)} %gather_fusion.2, bf16[2,4,128,512]{3,2,1,0:T(8,128)(2,1)} %gather_fusion.1, pred[2]{0:T(512)(128)(4,1)S(1)} %compare_and_fusion), kind=kOutput, calls=%fused_computation.18 | convolution fusion | flops 134742016 | bytes 2621442 | tf_op jit(solution)/shard_map/feik,efjk->efij/dot_general | solution.py:53
  60.0 0.2 reshape.130
  60.2 2.8 %gather_fusion.3 = f32[8,8,16384]{2,1,0:T(8,128)} fusion(f32[2,8,16384]{2,1,0:T(8,128)S(1)} %reshape.130, s32[1024]{0:T(1024)S(1)} %pad_clamp_fusion), kind=kCustom, calls=%fused_computation.3 | custom fusion | bytes 8388640 | tf_op jit(solution)/shard_map/jit(_take)/gather | solution.py:93
  63.1 4.6 %select_multiply_fusion = f32[4,2,8,16384]{3,2,1,0:T(8,128)} fusion(f32[4,2,8,16384]{3,2,1,0:T(8,128)} %bitcast.69, f32[4,2]{1,0:T(4,128)S(1)} %select_n.125, pred[4,2]{1,0:T(4,128)(4,1)S(1)} %compare_and_fusion.1), kind=kLoop, calls=%fused_computation.9 | loop fusion | flops 2097152 | bytes 8388648 | tf_op jit(solution)/shard_map/mul | solution.py:93
  67.7 5.1 %all-to-all-start = ((f32[4,2,8,16384]{3,2,1,0:T(8,128)}), f32[4,2,8,16384]{3,2,1,0:T(8,128)}, u32[]{:S(2)}, u32[]{:S(2)}) async-start(f32[4,2,8,16384]{3,2,1,0:T(8,128)} %select_multiply_fusion), calls=%async_computation | async-start | bytes 8388608 | tf_op jit(solution)/shard_map/all_to_all | solution.py:99
  72.8 0.1 multiply_sine_fusion
  73.0 87.6 %all-to-all-done = f32[4,2,8,16384]{3,2,1,0:T(8,128)} async-done(((f32[4,2,8,16384]{3,2,1,0:T(8,128)}), f32[4,2,8,16384]{3,2,1,0:T(8,128)}, u32[]{:S(2)}, u32[]{:S(2)}) %all-to-all-start) | async-done | bytes 4194336 | tf_op jit(solution)/shard_map/all_to_all | solution.py:99
  160.6 8.7 %convolution_bitcast_fusion = f32[2,64,16384]{2,1,0:T(8,128)S(1)} fusion(f32[4,8,64,1]{2,1,3,0:T(8,128)S(1)} %bitcast.75, f32[4,2,8,16384]{3,2,1,0:T(8,128)} %all-to-all-done), kind=kOutput, calls=%fused_computation.4 | convolution fusion | flops 805306368 | bytes 12591104 | tf_op jit(solution)/shard_map/pkgx,pgl->klx/dot_general | solution.py:97
  169.3 2.6 %fusion.1 = f32[2,32,16384]{2,1,0:T(8,128)} fusion(f32[2,64,16384]{2,1,0:T(8,128)S(1)} %convolution_bitcast_fusion), kind=kLoop, calls=%fused_computation.7 | loop fusion | flops 4194304 | bytes 12582912 | tf_op jit(solution)/shard_map/mul | solution.py:103
  (30 shorter events, 0.4 us)
Async XLA Ops:
  15.2 8.0 %copy-start = (f32[4,512,256]{2,1,0:T(8,128)S(1)}, f32[4,512,256]{2,1,0:T(8,128)}, u32[]{:S(2)}) copy-start(f32[4,512,256]{2,1,0:T(8,128)} %param.4) | copy-start | bytes 6291460
  23.2 12.0 %copy-start.5 = (s32[1,2,1]{1,2,0:T(1,128)S(1)}, s32[1,2,1]{1,2,0:T(1,128)}, u32[]{:S(2)}) copy-start(s32[1,2,1]{1,2,0:T(1,128)} %param.7) | copy-start | bytes 28
  23.3 12.3 %copy-start.3 = (s32[1,2,2]{2,1,0:T(2,128)S(1)}, s32[1,2,2]{2,1,0:T(2,128)}, u32[]{:S(2)}) copy-start(s32[1,2,2]{2,1,0:T(2,128)} %param.5) | copy-start | bytes 52
  23.3 12.4 %copy-start.4 = (s32[1,2]{1,0:T(1,128)S(1)}, s32[1,2]{1,0:T(1,128)}, u32[]{:S(2)}) copy-start(s32[1,2]{1,0:T(1,128)} %param.6) | copy-start | bytes 28
  33.2 13.9 %collective-permute-start = (bf16[4,128,512]{2,1,0:T(8,128)(2,1)}, bf16[4,128,512]{2,1,0:T(8,128)(2,1)}, u32[]{:S(2)}, u32[]{:S(2)}) collective-permute-start(bf16[4,128,512]{2,1,0:T(8,128)(2,1)} %get-tuple-element.9), channel_id=1, source_target_pairs={{0,12},{4,0},{8,4},{12,8},{1,13},{5,1},{9,5},{13,9},{2,14},{6,2},{... | collective-permute-start | bytes 1572872 | tf_op jit(solution)/shard_map/ppermute | solution.py:17
  34.9 18.6 %collective-permute-start.1 = (bf16[4,128,512]{2,1,0:T(8,128)(2,1)}, bf16[4,128,512]{2,1,0:T(8,128)(2,1)}, u32[]{:S(2)}, u32[]{:S(2)}) collective-permute-start(bf16[4,128,512]{2,1,0:T(8,128)(2,1)} %get-tuple-element.10), channel_id=1, source_target_pairs={{0,8},{4,12},{8,0},{12,4},{1,9},{5,13},{9,1},{13,5},{2,10},{6,14},... | collective-permute-start | bytes 1572872 | tf_op jit(solution)/shard_map/ppermute | solution.py:17
  37.3 2.9 %copy-start.1 = (bf16[4,4,128,512]{3,2,1,0:T(8,128)(2,1)S(1)}, bf16[4,4,128,512]{3,2,1,0:T(8,128)(2,1)}, u32[]{:S(2)}) copy-start(bf16[4,4,128,512]{3,2,1,0:T(8,128)(2,1)} %pad_maximum_fusion) | copy-start | bytes 6291460
  41.9 14.5 %copy-start.2 = (bf16[2,4,128,512]{3,2,1,0:T(8,128)(2,1)S(1)}, bf16[2,4,128,512]{3,2,1,0:T(8,128)(2,1)}, u32[]{:S(2)}) copy-start(bf16[2,4,128,512]{3,2,1,0:T(8,128)(2,1)} %gather_fusion) | copy-start | bytes 3145732
  67.7 92.9 %all-to-all-start = ((f32[4,2,8,16384]{3,2,1,0:T(8,128)}), f32[4,2,8,16384]{3,2,1,0:T(8,128)}, u32[]{:S(2)}, u32[]{:S(2)}) async-start(f32[4,2,8,16384]{3,2,1,0:T(8,128)} %select_multiply_fusion), calls=%async_computation | async-start | bytes 8388608 | tf_op jit(solution)/shard_map/all_to_all | solution.py:99
where the time goes:
time: 172 us
  waiting for transfers between devices  96.9 us (56%)
  other arithmetic  30.9 us (18%)
  matrix products  12.2 us (7%)
  blocking collectives  11.6 us (7%)
  local copies, waits for them, and re-layouts  9.09 us (5%)
  starting transfers between devices  7.08 us (4%)
  between operations  4.2 us (2%)
    all_to_all x1, waiting for transfers between devices, on_device(): lax.all_to_all(outgoing, 'freq', split_axis=0, concat_axis=0, tiled=True)  87.6 us
    ppermute x2, waiting for transfers between devices, from_behind(): return lax.ppermute(x, axis, [(i, (i + by) % count) for i in range(count)])  9.31 us
    dot_general x1, matrix products, on_device(): jnp.einsum('pkgx,pgl->klx', lax.all_to_all(outgoing, 'freq', split_axis=0...  8.7 us
    another operation x1, other arithmetic  7.97 us
    neg x1, other arithmetic, on_device(): -home_block[..., :seg_count]  7.55 us
    all_gather x1, blocking collectives, on_device(): lax.all_gather(block_offsets, 'chan', axis=0, tiled=True)  6.13 us
    all_gather x1, blocking collectives, on_device(): lax.all_gather(tile_pairs, 'chan', axis=0, tiled=True)  5.48 us
    all_to_all x1, starting transfers between devices, on_device(): lax.all_to_all(outgoing, 'freq', split_axis=0, concat_axis=0, tiled=True)  5.13 us
  transfers between devices with their start and end apart: 3, of which 3 were waited for; matrix products, arithmetic and copies ran while one was open for 5% of the time, Pallas kernels for 0%

commit v1 on v0

v1 whole, which is shorter than its diff:
```python
import functools
import math

import jax
import jax.numpy as jnp
import numpy as np
from jax import lax
from jax.experimental import pallas as pl
from jax.experimental.pallas import tpu as pltpu
from jax.sharding import PartitionSpec as P

F = 16
NFFT = 512
TILE = 128
CAP = 2
LAGS = 32
ROW_STEP = 32
MESH = pl.DeviceIdType.MESH

SIN_TERMS = (
    0.999999999982969,
    -0.16666666616916945,
    0.008333330977498568,
    -0.00019840861553013607,
    2.752528712920731e-06,
    -2.3889498620743105e-08,
)
COS_TERMS = (
    0.99999999999925,
    -0.4999999999701845,
    0.04166666647312386,
    -0.0013888884175533636,
    2.4801040301795323e-05,
    -2.752468399134539e-07,
    1.9907690634373785e-09,
)


def polynomial(terms, u):
    total = jnp.full_like(u, terms[-1])
    for term in terms[-2::-1]:
        total = total * u + term
    return total


def cos_sin(x):
    half = x * 0.5
    u = half * half
    s = half * polynomial(SIN_TERMS, u)
    c = polynomial(COS_TERMS, u)
    twice = s + s
    return 1.0 - twice * s, twice * c


def lag_table():
    bins = np.arange(F, dtype=np.float64) + 32.0
    lag_index = np.arange(LAGS, dtype=np.float64) - float(LAGS // 2)
    angles = 2.0 * math.pi / NFFT * bins[:, None] * lag_index[None, :]
    cosine, sine = np.cos(angles), np.sin(angles)
    real_rows = np.concatenate([cosine, sine], axis=1)
    imag_rows = np.concatenate([-sine, cosine], axis=1)
    return np.stack([real_rows, imag_rows], axis=1).reshape(2 * F, 2 * LAGS)


def split_table():
    table = lag_table().T
    high = table.astype(np.float32).astype(jnp.bfloat16)
    low = (table - high.astype(np.float64)).astype(np.float32).astype(jnp.bfloat16)
    return np.concatenate([high, low], axis=1)


def gather_kernel(
    loop,
    line,
    pairs_ref,
    offsets_ref,
    phases_ref,
    all_ref,
    want,
    asked,
    spec,
    going,
    coming,
    own,
    want_send,
    want_recv,
    tile_send,
    tile_recv,
    line_send,
    line_recv,
    local_sem,
):
    me = lax.axis_index("chan")
    pos = lax.axis_index("freq")
    freq_local, block_width, seg_count = phases_ref.shape
    steps = want.shape[0]
    list_len = offsets_ref.shape[1]

    def at_chan(delta):
        return {"chan": lax.rem(me + (delta % loop), loop)}

    def at_freq(delta):
        return {"freq": lax.rem(pos + (delta % line), line)}

    chan_deltas = sorted(
        {(sign * (o + 1)) % loop for o in range(steps) for sign in (1, -1)} - {0}
    )
    freq_deltas = sorted({1 % line, -1 % line} - {0})
    barrier = pltpu.get_barrier_semaphore()
    for delta in chan_deltas:
        pl.semaphore_signal(barrier, inc=1, device_id=at_chan(delta), device_id_type=MESH)
    for delta in freq_deltas:
        pl.semaphore_signal(barrier, inc=1, device_id=at_freq(delta), device_id_type=MESH)
    pl.semaphore_wait(barrier, len(chan_deltas) + len(freq_deltas))

    left_tiles = []
    want_copies = []
    for o in range(steps):
        row_tile = jnp.int32(0)
        col_tile = jnp.int32(0)
        for e in range(list_len):
            here = offsets_ref[0, e] == o
            row_tile = row_tile + jnp.where(here, pairs_ref[0, e, 0], 0)
            col_tile = col_tile + jnp.where(here, pairs_ref[0, e, 1], 0)
        left_tiles.append(row_tile)
        want[o] = jnp.full(want.shape[1:], col_tile, jnp.int32)
        copy = pltpu.make_async_remote_copy(
            src_ref=want.at[o],
            dst_ref=asked.at[o],
            send_sem=want_send.at[o],
            recv_sem=want_recv.at[o],
            device_id=at_chan(o + 1),
            device_id_type=MESH,
        )
        copy.start()
        want_copies.append(copy)

    def tile_of(f, index):
        chosen = spec[f, 0:TILE, :]
        for t in range(1, block_width // TILE):
            chosen = jnp.where(index == t, spec[f, t * TILE : (t + 1) * TILE, :], chosen)
        return chosen

    tile_copies = {}
    asked_tiles = []
    for f in range(freq_local):

        @pl.loop(0, block_width // ROW_STEP)
        def _(step):
            rows = pl.ds(pl.multiple_of(step * ROW_STEP, ROW_STEP), ROW_STEP)
            c, s = cos_sin(phases_ref[f, rows, :])
            spec[f, rows, 0:seg_count] = c.astype(jnp.bfloat16)
            spec[f, rows, seg_count:] = s.astype(jnp.bfloat16)

        if f == 0:
            for o in range(steps):
                want_copies[o].wait_recv()
                asked_tiles.append(jnp.max(asked[o]))
        for o in range(steps):
            going[o, f] = tile_of(f, asked_tiles[o])
            copy = pltpu.make_async_remote_copy(
                src_ref=going.at[o, f],
                dst_ref=coming.at[o, f],
                send_sem=tile_send.at[o, f],
                recv_sem=tile_recv.at[o, f],
                device_id=at_chan(-(o + 1)),
                device_id_type=MESH,
            )
            copy.start()
            tile_copies[o, f] = copy

    units = [(o, f) for f in range(freq_local) for o in range(steps)]

    def line_copy(right, stage, unit, origin, source=None):
        o, f = units[unit]
        place = all_ref.at[o, origin, f]
        way = 0 if right else 1
        return pltpu.make_async_remote_copy(
            src_ref=place if source is None else source,
            dst_ref=place,
            send_sem=line_send.at[way, stage, unit],
            recv_sem=line_recv.at[way, stage, unit],
            device_id=at_freq(1 if right else -1),
            device_id_type=MESH,
        )

    def can_send(right):
        return pos < line - 1 if right else pos > 0

    def arrives(right, stage):
        return pos - (stage + 1) >= 0 if right else pos + (stage + 1) <= line - 1

    def origin_at(right, stage):
        return pos - stage if right else pos + stage

    def take_and_forward(stage, unit):
        for right in (True, False):

            @pl.when(arrives(right, stage))
            def _():
                origin = origin_at(right, stage + 1)
                line_copy(right, stage, unit, origin).wait_recv()
                if stage + 1 < line - 1:

                    @pl.when(can_send(right))
                    def _():
                        line_copy(right, stage + 1, unit, origin).start()

    local_copies = []
    for turn in range(len(units) + line - 1):
        if turn < len(units):
            o, f = units[turn]
            tile_copies[o, f].wait_recv()
            left = tile_of(f, left_tiles[o])
            swapped = jnp.concatenate(
                [left[:, seg_count:], -left[:, :seg_count]], axis=1
            )
            products = lax.dot_general(
                jnp.concatenate([left, swapped], axis=0),
                coming[o, f],
                (((1,), (1,)), ((), ())),
                preferred_element_type=jnp.float32,
            )
            own[o, f, 0] = products[:TILE].astype(own.dtype)
            own[o, f, 1] = products[TILE:].astype(own.dtype)
            for right in (True, False):

                @pl.when(can_send(right))
                def _():
                    line_copy(right, 0, turn, pos, own.at[o, f]).start()

            copy = pltpu.make_async_copy(
                own.at[o, f], all_ref.at[o, pos, f], local_sem.at[turn]
            )
            copy.start()
            local_copies.append(copy)
        for stage in range(line - 1):
            unit = turn - 1 - stage
            if 0 <= unit < len(units):
                take_and_forward(stage, unit)

    for copy in local_copies:
        copy.wait()
    for copy in want_copies:
        copy.wait_send()
    for copy in tile_copies.values():
        copy.wait_send()
    for unit, (o, f) in enumerate(units):
        for right in (True, False):

            @pl.when(can_send(right))
            def _():
                line_copy(right, 0, unit, pos, own.at[o, f]).wait_send()
                for stage in range(line - 2):

                    @pl.when(arrives(right, stage))
                    def _():
                        origin = origin_at(right, stage + 1)
                        line_copy(right, stage + 1, unit, origin).wait_send()


def slot_of(slot, owners_ref, offsets_ref, place_ref):
    earlier, chosen, found = jnp.int32(0), jnp.int32(0), jnp.int32(0)
    for e in range(offsets_ref.shape[0]):
        mine = owners_ref[e] == place_ref[0]
        hit = jnp.logical_and(mine, earlier == slot)
        chosen = jnp.where(hit, offsets_ref[e], chosen)
        found = jnp.where(hit, 1, found)
        earlier = earlier + jnp.where(mine, 1, 0)
    return chosen, found


def lag_kernel(
    env_scale, owners_ref, offsets_ref, place_ref, table_ref, cross_ref, out_ref, by_row
):
    _, parts, rows, width = cross_ref.shape
    _, found = slot_of(pl.program_id(0), owners_ref, offsets_ref, place_ref)
    scale = jnp.where(found == 1, jnp.float32(env_scale), jnp.float32(0.0))
    for k in range(parts):
        by_row[pl.ds(k, rows, stride=parts), :] = cross_ref[0, k].astype(jnp.float32)
    table = table_ref[...]
    for i in range(0, rows, 2):
        pair = jnp.concatenate(
            [
                by_row[pl.ds(i * parts, parts), :],
                by_row[pl.ds((i + 1) * parts, parts), :],
            ],
            axis=1,
        ).astype(jnp.bfloat16)
        lagged = jnp.dot(
            table,
            jnp.concatenate([pair, pair], axis=0),
            preferred_element_type=jnp.float32,
        )
        real, imag = lagged[:LAGS], lagged[LAGS:]
        out_ref[0, :, pl.ds(i * width, 2 * width)] = (real * real + imag * imag) * scale


def on_device(loop, line, phases, tile_pairs, block_offsets, owners):
    freq_local, block_width, seg_count = phases.shape
    steps = loop // 2
    units = steps * freq_local
    list_len = block_offsets.shape[1]
    parts = line * freq_local * 2
    both = 2 * seg_count
    gathered = pl.pallas_call(
        functools.partial(gather_kernel, loop, line),
        out_shape=jax.ShapeDtypeStruct(
            (steps, line, freq_local, 2, TILE, TILE), jnp.bfloat16
        ),
        in_specs=[
            pl.BlockSpec(memory_space=pltpu.SMEM),
            pl.BlockSpec(memory_space=pltpu.SMEM),
            pl.BlockSpec(memory_space=pltpu.VMEM),
        ],
        out_specs=pl.BlockSpec(memory_space=pl.ANY),
        scratch_shapes=[
            pltpu.VMEM((steps, 8, 128), jnp.int32),
            pltpu.VMEM((steps, 8, 128), jnp.int32),
            pltpu.VMEM((freq_local, block_width, both), jnp.bfloat16),
            pltpu.VMEM((steps, freq_local, TILE, both), jnp.bfloat16),
            pltpu.VMEM((steps, freq_local, TILE, both), jnp.bfloat16),
            pltpu.VMEM((steps, freq_local, 2, TILE, TILE), jnp.bfloat16),
            pltpu.SemaphoreType.DMA((steps,)),
            pltpu.SemaphoreType.DMA((steps,)),
            pltpu.SemaphoreType.DMA((steps, freq_local)),
            pltpu.SemaphoreType.DMA((steps, freq_local)),
            pltpu.SemaphoreType.DMA((2, line - 1, units)),
            pltpu.SemaphoreType.DMA((2, line - 1, units)),
            pltpu.SemaphoreType.DMA((units,)),
        ],
        compiler_params=pltpu.CompilerParams(
            collective_id=0, has_side_effects=True, vmem_limit_bytes=32 * 2**20
        ),
        name="gather_products",
    )(tile_pairs, block_offsets, phases)

    rows = 32
    place = lax.axis_index("freq").astype(jnp.int32).reshape(1)

    def cross_block(slot, part, *refs):
        return slot_of(slot, *refs)[0], 0, part, 0

    return pl.pallas_call(
        functools.partial(lag_kernel, 1.0 / (F * seg_count)),
        out_shape=jax.ShapeDtypeStruct((CAP, LAGS, TILE * TILE), jnp.float32),
        grid_spec=pltpu.PrefetchScalarGridSpec(
            num_scalar_prefetch=3,
            grid=(CAP, TILE // rows),
            in_specs=[
                pl.BlockSpec((2 * LAGS, 2 * parts), lambda *_: (0, 0)),
                pl.BlockSpec((1, parts, rows, TILE), cross_block),
            ],
            out_specs=pl.BlockSpec(
                (1, LAGS, rows * TILE), lambda slot, part, *_: (slot, 0, part)
            ),
            scratch_shapes=[pltpu.VMEM((rows * parts, TILE), jnp.float32)],
        ),
        compiler_params=pltpu.CompilerParams(vmem_limit_bytes=24 * 2**20),
        name="lag_sums",
    )(
        owners.reshape(list_len),
        block_offsets.reshape(list_len),
        place,
        jnp.asarray(split_table()),
        gathered.reshape(steps, parts, TILE, TILE),
    )


def solution(mesh):
    in_specs = (
        P(("grp", "freq"), "chan", None),
        P("chan", None, None),
        P("chan", None),
        P("chan", None, None),
    )
    out_specs = P(("grp", "chan", "freq"), None, None)
    return jax.shard_map(
        functools.partial(on_device, mesh.shape["chan"], mesh.shape["freq"]),
        mesh=mesh,
        in_specs=in_specs,
        out_specs=out_specs,
        check_vma=False,
    )
```

time: 172 us -> 60.7 us (0.35)
  waiting for transfers between devices: 96.9 us -> 0 us
  Pallas kernels: 0 us -> 57.6 us
  other arithmetic: 30.9 us -> 0 us
  matrix products: 12.2 us -> 0 us
  blocking collectives: 11.6 us -> 0 us
  starting transfers between devices: 7.08 us -> 0 us
  local copies, waits for them, and re-layouts: 9.09 us -> 2.93 us
  between operations: 4.2 us -> 0.03 us
    all_to_all x1 -> x0, waiting for transfers between devices: 87.6 us -> none  [on_device(): lax.all_to_all(outgoing, 'freq', split_axis=0, concat_axis=0, tiled=True)]
    pallas_call x0 -> x2, Pallas kernels: none -> 57.6 us  [the longest x1 50.7 us: on_device(): pl.pallas_call(functools.partial(gather_kernel, loop, line), out_shape=ja...]
    dot_general x3 -> x0, matrix products: 12.2 us -> none  [the longest x1 8.7 us: on_device(): jnp.einsum('pkgx,pgl->klx', lax.all_to_all(outgoing, 'freq', split_axis=0...]
    all_gather x2 -> x0, blocking collectives: 11.6 us -> none  [the longest x1 6.13 us: on_device(): lax.all_gather(block_offsets, 'chan', axis=0, tiled=True)]
    another operation x4 -> x0, other arithmetic: 9.36 us -> none
    ppermute x2 -> x0, waiting for transfers between devices: 9.31 us -> none  [from_behind(): return lax.ppermute(x, axis, [(i, (i + by) % count) for i in range(count)])]
    gather x4 -> x0, local copies, waits for them, and re-layouts: 8.31 us -> none  [the longest x1 2.83 us: on_device(): outgoing = jnp.take(cross_tiles, entries, axis=0) * filled[:, None, None]]
    neg x1 -> x0, other arithmetic: 7.55 us -> none  [on_device(): -home_block[..., :seg_count]]
  transfers between devices with their start and end apart: 3 -> 0, of which waited for: 3 -> 0; matrix products, arithmetic and copies ran while one was open for 5% -> 0% of each run, Pallas kernels for 0% -> 0%
where the time goes in v1:
time: 60.7 us; the launch traced here: 60.5 us
  Pallas kernels  57.6 us (95%)
  local copies, waits for them, and re-layouts  2.93 us (5%)
    pallas_call x1, Pallas kernels, on_device(): pl.pallas_call(functools.partial(gather_kernel, loop, line), out_shape=ja...  50.7 us
    pallas_call x1, Pallas kernels, on_device(): pl.pallas_call(functools.partial(lag_kernel, 1.0 / (F * seg_count)), out_...  6.9 us
    unnamed x10, local copies, waits for them, and re-layouts  2.93 us

profile of v1, /device:TPU:0, one launch (start us, length us, event | category | flops | bytes accessed | tf_op | source)
XLA Modules:
  0.0 60.5 jit_solution(1436447281492615913)
XLA Ops:
  0.0 0.0 copy-start
  0.0 1.6 %copy-done = f32[4,512,256]{2,1,0:T(8,128)S(1)} copy-done((f32[4,512,256]{2,1,0:T(8,128)S(1)}, f32[4,512,256]{2,1,0:T(8,128)}, u32[]{:S(2)}) %copy-start) | copy-done | bytes 2097176
  1.6 0.0 copy-start.2
  1.6 0.7 %copy-done.2 = s32[1,2]{1,0:T(1,128)S(1)} copy-done((s32[1,2]{1,0:T(1,128)S(1)}, s32[1,2]{1,0:T(1,128)}, u32[]{:S(2)}) %copy-start.2) | copy-done | bytes 32
  2.2 0.0 copy-start.3
  2.2 0.7 %copy-done.3 = s32[1,2,2]{2,1,0:T(2,128)S(1)} copy-done((s32[1,2,2]{2,1,0:T(2,128)S(1)}, s32[1,2,2]{2,1,0:T(2,128)}, u32[]{:S(2)}) %copy-start.3) | copy-done | bytes 40
  2.9 0.0 copy-start.1
  2.9 0.0 copy-start.4
  2.9 50.7 %gather_products.1 = bf16[2,4,4,2,128,128]{5,4,3,2,1,0:T(8,128)(2,1)S(1)} custom-call(s32[1,2,2]{2,1,0:T(2,128)S(1)} %copy-done.3, s32[1,2]{1,0:T(1,128)S(1)} %copy-done.2, f32[4,512,256]{2,1,0:T(8,128)S(1)} %copy-done), custom_call_target="tpu_custom_call" | custom-call | tf_op jit(solution)/shard_map/gather_products/pallas_call | solution.py:306
  53.6 0.0 copy-done.1
  53.6 0.0 copy-done.4
  53.6 6.9 %lag_sums.1 = f32[2,32,16384]{2,1,0:T(8,128)} custom-call(s32[2]{0:T(128)S(1)} %bitcast.6, s32[2]{0:T(128)S(1)} %bitcast.5, s32[1]{0:T(128)} %bitcast.2.place_ref, bf16[64,64]{1,0:T(8,128)(2,1)S(1)} %copy-done.1, bf16[2,32,128,128]{3,2,1,0:T(8,128)(2,1)S(1)} %bitcast.4), custom_call_target="tpu_custom_call" | custom-call | tf_op jit(solution)/shard_map/lag_sums/pallas_call | solution.py:344
Async XLA Ops:
  0.0 1.6 %copy-start = (f32[4,512,256]{2,1,0:T(8,128)S(1)}, f32[4,512,256]{2,1,0:T(8,128)}, u32[]{:S(2)}) copy-start(f32[4,512,256]{2,1,0:T(8,128)} %phases_ref.1) | copy-start | bytes 6291460
  1.6 0.7 %copy-start.2 = (s32[1,2]{1,0:T(1,128)S(1)}, s32[1,2]{1,0:T(1,128)}, u32[]{:S(2)}) copy-start(s32[1,2]{1,0:T(1,128)} %offsets_ref.1) | copy-start | bytes 28
  2.2 0.7 %copy-start.3 = (s32[1,2,2]{2,1,0:T(2,128)S(1)}, s32[1,2,2]{2,1,0:T(2,128)}, u32[]{:S(2)}) copy-start(s32[1,2,2]{2,1,0:T(2,128)} %pairs_ref.1) | copy-start | bytes 52
  2.9 50.7 %copy-start.1 = (bf16[64,64]{1,0:T(8,128)(2,1)S(1)}, bf16[64,64]{1,0:T(8,128)(2,1)}, u32[]{:S(2)}) copy-start(bf16[64,64]{1,0:T(8,128)(2,1)} %constant.6.clone.table_ref) | copy-start | bytes 24580
  2.9 50.7 %copy-start.4 = (s32[1,2,1]{1,2,0:T(1,128)S(1)}, s32[1,2,1]{1,2,0:T(1,128)}, u32[]{:S(2)}) copy-start(s32[1,2,1]{1,2,0:T(1,128)} %param.8) | copy-start | bytes 28

commit v2 on v1

--- a/solution.py
+++ b/solution.py
@@ -15,6 +15,7 @@
 CAP = 2
 LAGS = 32
 ROW_STEP = 32
+SUBLANES = 16
 MESH = pl.DeviceIdType.MESH
 
 SIN_TERMS = (
@@ -62,26 +63,35 @@
     return np.stack([real_rows, imag_rows], axis=1).reshape(2 * F, 2 * LAGS)
 
 
-def split_table():
-    table = lag_table().T
-    high = table.astype(np.float32).astype(jnp.bfloat16)
-    low = (table - high.astype(np.float64)).astype(np.float32).astype(jnp.bfloat16)
+def row_table(parts, rows):
+    table = lag_table().reshape(2 * F // parts, parts, 2 * LAGS)
+    spread = np.einsum("ab,ukl->alubk", np.eye(rows), table)
+    spread = spread.reshape(rows * 2 * LAGS, 2 * F * rows)
+    high = spread.astype(np.float32).astype(jnp.bfloat16)
+    low = (spread - high.astype(np.float64)).astype(np.float32).astype(jnp.bfloat16)
     return np.concatenate([high, low], axis=1)
 
 
 def gather_kernel(
     loop,
     line,
+    group,
+    halves,
+    pairs_hbm,
+    offsets_hbm,
+    phases_hbm,
+    all_ref,
     pairs_ref,
     offsets_ref,
     phases_ref,
-    all_ref,
     want,
     asked,
     spec,
     going,
     coming,
+    mixed,
     own,
+    in_sem,
     want_send,
     want_recv,
     tile_send,
@@ -96,6 +106,15 @@
     steps = want.shape[0]
     list_len = offsets_ref.shape[1]
 
+    sources = [(pairs_hbm, pairs_ref), (offsets_hbm, offsets_ref)]
+    sources += [(phases_hbm.at[f], phases_ref.at[f]) for f in range(freq_local)]
+    fetched = [
+        pltpu.make_async_copy(source, target, in_sem.at[n])
+        for n, (source, target) in enumerate(sources)
+    ]
+    for copy in fetched:
+        copy.start()
+
     def at_chan(delta):
         return {"chan": lax.rem(me + (delta % loop), loop)}
 
@@ -112,6 +131,9 @@
     for delta in freq_deltas:
         pl.semaphore_signal(barrier, inc=1, device_id=at_freq(delta), device_id_type=MESH)
     pl.semaphore_wait(barrier, len(chan_deltas) + len(freq_deltas))
+
+    fetched[0].wait()
+    fetched[1].wait()
 
     left_tiles = []
     want_copies = []
@@ -143,37 +165,45 @@
 
     tile_copies = {}
     asked_tiles = []
-    for f in range(freq_local):
-
-        @pl.loop(0, block_width // ROW_STEP)
-        def _(step):
-            rows = pl.ds(pl.multiple_of(step * ROW_STEP, ROW_STEP), ROW_STEP)
-            c, s = cos_sin(phases_ref[f, rows, :])
-            spec[f, rows, 0:seg_count] = c.astype(jnp.bfloat16)
-            spec[f, rows, seg_count:] = s.astype(jnp.bfloat16)
-
-        if f == 0:
-            for o in range(steps):
+    for g in range(freq_local // group):
+        for f in range(g * group, (g + 1) * group):
+            fetched[2 + f].wait()
+
+            @pl.loop(0, block_width // ROW_STEP)
+            def _(step):
+                rows = pl.ds(pl.multiple_of(step * ROW_STEP, ROW_STEP), ROW_STEP)
+                c, s = cos_sin(phases_ref[f, rows, :])
+                spec[f, rows, 0:seg_count] = c.astype(jnp.bfloat16)
+                spec[f, rows, seg_count:] = s.astype(jnp.bfloat16)
+
+        for o in range(steps):
+            if g == 0:
                 want_copies[o].wait_recv()
                 asked_tiles.append(jnp.max(asked[o]))
-        for o in range(steps):
-            going[o, f] = tile_of(f, asked_tiles[o])
-            copy = pltpu.make_async_remote_copy(
-                src_ref=going.at[o, f],
-                dst_ref=coming.at[o, f],
-                send_sem=tile_send.at[o, f],
-                recv_sem=tile_recv.at[o, f],
-                device_id=at_chan(-(o + 1)),
-                device_id_type=MESH,
-            )
-            copy.start()
-            tile_copies[o, f] = copy
-
-    units = [(o, f) for f in range(freq_local) for o in range(steps)]
+            for f in range(g * group, (g + 1) * group):
+                going[o, f] = tile_of(f, asked_tiles[o])
+                copy = pltpu.make_async_remote_copy(
+                    src_ref=going.at[o, f],
+                    dst_ref=coming.at[o, f],
+                    send_sem=tile_send.at[o, f],
+                    recv_sem=tile_recv.at[o, f],
+                    device_id=at_chan(-(o + 1)),
+                    device_id_type=MESH,
+                )
+                copy.start()
+                tile_copies[o, f] = copy
+
+    units = [
+        (o, g, h)
+        for g in range(freq_local // group)
+        for o in range(steps)
+        for h in range(halves)
+    ]
+    part_rows = TILE * 2 * group // halves
 
     def line_copy(right, stage, unit, origin, source=None):
-        o, f = units[unit]
-        place = all_ref.at[o, origin, f]
+        o, g, h = units[unit]
+        place = all_ref.at[o, origin, g, h]
         way = 0 if right else 1
         return pltpu.make_async_remote_copy(
             src_ref=place if source is None else source,
@@ -209,28 +239,33 @@
     local_copies = []
     for turn in range(len(units) + line - 1):
         if turn < len(units):
-            o, f = units[turn]
-            tile_copies[o, f].wait_recv()
-            left = tile_of(f, left_tiles[o])
-            swapped = jnp.concatenate(
-                [left[:, seg_count:], -left[:, :seg_count]], axis=1
-            )
-            products = lax.dot_general(
-                jnp.concatenate([left, swapped], axis=0),
-                coming[o, f],
-                (((1,), (1,)), ((), ())),
-                preferred_element_type=jnp.float32,
-            )
-            own[o, f, 0] = products[:TILE].astype(own.dtype)
-            own[o, f, 1] = products[TILE:].astype(own.dtype)
+            o, g, h = units[turn]
+            if h == 0:
+                for n in range(group):
+                    f = g * group + n
+                    tile_copies[o, f].wait_recv()
+                    left = tile_of(f, left_tiles[o])
+                    swapped = jnp.concatenate(
+                        [left[:, seg_count:], -left[:, :seg_count]], axis=1
+                    )
+                    products = lax.dot_general(
+                        jnp.concatenate([left, swapped], axis=0),
+                        coming[o, f],
+                        (((1,), (1,)), ((), ())),
+                        preferred_element_type=jnp.float32,
+                    )
+                    stride = 2 * group
+                    mixed[pl.ds(2 * n, TILE, stride=stride), :] = products[:TILE]
+                    mixed[pl.ds(2 * n + 1, TILE, stride=stride), :] = products[TILE:]
+            own[o, g, h] = mixed[h * part_rows : (h + 1) * part_rows, :].astype(own.dtype)
             for right in (True, False):
 
                 @pl.when(can_send(right))
                 def _():
-                    line_copy(right, 0, turn, pos, own.at[o, f]).start()
+                    line_copy(right, 0, turn, pos, own.at[o, g, h]).start()
 
             copy = pltpu.make_async_copy(
-                own.at[o, f], all_ref.at[o, pos, f], local_sem.at[turn]
+                own.at[o, g, h], all_ref.at[o, pos, g, h], local_sem.at[turn]
             )
             copy.start()
             local_copies.append(copy)
@@ -245,12 +280,12 @@
         copy.wait_send()
     for copy in tile_copies.values():
         copy.wait_send()
-    for unit, (o, f) in enumerate(units):
+    for unit, (o, g, h) in enumerate(units):
         for right in (True, False):
 
             @pl.when(can_send(right))
             def _():
-                line_copy(right, 0, unit, pos, own.at[o, f]).wait_send()
+                line_copy(right, 0, unit, pos, own.at[o, g, h]).wait_send()
                 for stage in range(line - 2):
 
                     @pl.when(arrives(right, stage))
@@ -271,56 +306,66 @@
 
 
 def lag_kernel(
-    env_scale, owners_ref, offsets_ref, place_ref, table_ref, cross_ref, out_ref, by_row
+    env_scale, owners_ref, offsets_ref, place_ref, table_ref, cross_ref, out_ref
 ):
-    _, parts, rows, width = cross_ref.shape
+    _, groups, block_rows, width = cross_ref.shape
     _, found = slot_of(pl.program_id(0), owners_ref, offsets_ref, place_ref)
     scale = jnp.where(found == 1, jnp.float32(env_scale), jnp.float32(0.0))
-    for k in range(parts):
-        by_row[pl.ds(k, rows, stride=parts), :] = cross_ref[0, k].astype(jnp.float32)
     table = table_ref[...]
-    for i in range(0, rows, 2):
-        pair = jnp.concatenate(
-            [
-                by_row[pl.ds(i * parts, parts), :],
-                by_row[pl.ds((i + 1) * parts, parts), :],
-            ],
-            axis=1,
-        ).astype(jnp.bfloat16)
+    rows_at_once = table.shape[0] // (2 * LAGS)
+
+    def stacked(at):
+        start = at * SUBLANES
+        return jnp.concatenate(
+            [cross_ref[0, u, start : start + SUBLANES, :] for u in range(groups)], axis=0
+        )
+
+    for at in range(0, block_rows // SUBLANES, 2):
+        pair = jnp.concatenate([stacked(at), stacked(at + 1)], axis=1)
         lagged = jnp.dot(
             table,
             jnp.concatenate([pair, pair], axis=0),
             preferred_element_type=jnp.float32,
         )
-        real, imag = lagged[:LAGS], lagged[LAGS:]
-        out_ref[0, :, pl.ds(i * width, 2 * width)] = (real * real + imag * imag) * scale
+        for i in range(rows_at_once):
+            start = i * 2 * LAGS
+            real = lagged[start : start + LAGS]
+            imag = lagged[start + LAGS : start + 2 * LAGS]
+            envelope = (real * real + imag * imag) * scale
+            for n in range(2):
+                place = ((at + n) * rows_at_once + i) * width
+                out_ref[0, :, place : place + width] = envelope[:, n * width : (n + 1) * width]
 
 
 def on_device(loop, line, phases, tile_pairs, block_offsets, owners):
     freq_local, block_width, seg_count = phases.shape
     steps = loop // 2
-    units = steps * freq_local
+    group = 2 if freq_local % 2 == 0 else 1
+    halves = 2
+    groups = freq_local // group
+    units = steps * groups * halves
+    part_rows = TILE * 2 * group // halves
     list_len = block_offsets.shape[1]
-    parts = line * freq_local * 2
     both = 2 * seg_count
     gathered = pl.pallas_call(
-        functools.partial(gather_kernel, loop, line),
+        functools.partial(gather_kernel, loop, line, group, halves),
         out_shape=jax.ShapeDtypeStruct(
-            (steps, line, freq_local, 2, TILE, TILE), jnp.bfloat16
+            (steps, line, groups, halves, part_rows, TILE), jnp.bfloat16
         ),
-        in_specs=[
-            pl.BlockSpec(memory_space=pltpu.SMEM),
-            pl.BlockSpec(memory_space=pltpu.SMEM),
-            pl.BlockSpec(memory_space=pltpu.VMEM),
-        ],
+        in_specs=[pl.BlockSpec(memory_space=pltpu.HBM)] * 3,
         out_specs=pl.BlockSpec(memory_space=pl.ANY),
         scratch_shapes=[
+            pltpu.SMEM(tile_pairs.shape, jnp.int32),
+            pltpu.SMEM(block_offsets.shape, jnp.int32),
+            pltpu.VMEM(phases.shape, jnp.float32),
             pltpu.VMEM((steps, 8, 128), jnp.int32),
             pltpu.VMEM((steps, 8, 128), jnp.int32),
             pltpu.VMEM((freq_local, block_width, both), jnp.bfloat16),
             pltpu.VMEM((steps, freq_local, TILE, both), jnp.bfloat16),
             pltpu.VMEM((steps, freq_local, TILE, both), jnp.bfloat16),
-            pltpu.VMEM((steps, freq_local, 2, TILE, TILE), jnp.bfloat16),
+            pltpu.VMEM((TILE * 2 * group, TILE), jnp.float32),
+            pltpu.VMEM((steps, groups, halves, part_rows, TILE), jnp.bfloat16),
+            pltpu.SemaphoreType.DMA((2 + freq_local,)),
             pltpu.SemaphoreType.DMA((steps,)),
             pltpu.SemaphoreType.DMA((steps,)),
             pltpu.SemaphoreType.DMA((steps, freq_local)),
@@ -330,12 +375,13 @@
             pltpu.SemaphoreType.DMA((units,)),
         ],
         compiler_params=pltpu.CompilerParams(
-            collective_id=0, has_side_effects=True, vmem_limit_bytes=32 * 2**20
+            collective_id=0, has_side_effects=True, vmem_limit_bytes=58 * 2**20
         ),
         name="gather_products",
     )(tile_pairs, block_offsets, phases)
 
     rows = 32
+    table = row_table(2 * group, SUBLANES // (2 * group))
     place = lax.axis_index("freq").astype(jnp.int32).reshape(1)
 
     def cross_block(slot, part, *refs):
@@ -348,13 +394,12 @@
             num_scalar_prefetch=3,
             grid=(CAP, TILE // rows),
             in_specs=[
-                pl.BlockSpec((2 * LAGS, 2 * parts), lambda *_: (0, 0)),
-                pl.BlockSpec((1, parts, rows, TILE), cross_block),
+                pl.BlockSpec(table.shape, lambda *_: (0, 0)),
+                pl.BlockSpec((1, line * groups, rows * 2 * group, TILE), cross_block),
             ],
             out_specs=pl.BlockSpec(
                 (1, LAGS, rows * TILE), lambda slot, part, *_: (slot, 0, part)
             ),
-            scratch_shapes=[pltpu.VMEM((rows * parts, TILE), jnp.float32)],
         ),
         compiler_params=pltpu.CompilerParams(vmem_limit_bytes=24 * 2**20),
         name="lag_sums",
@@ -362,8 +407,8 @@
         owners.reshape(list_len),
         block_offsets.reshape(list_len),
         place,
-        jnp.asarray(split_table()),
-        gathered.reshape(steps, parts, TILE, TILE),
+        jnp.asarray(table),
+        gathered.reshape(steps, line * groups, TILE * 2 * group, TILE),
     )
 
 

time: 60.7 us -> 58.8 us (0.969)
  local copies, waits for them, and re-layouts: 2.93 us -> 1.6 us
    pallas_call x1, Pallas kernels: 6.9 us -> 5.44 us  [on_device(): pl.pallas_call(functools.partial(lag_kernel, 1.0 / (F * seg_count)), out_...]
    unnamed x10 -> x8, local copies, waits for them, and re-layouts: 2.93 us -> 1.6 us
    pallas_call x1, Pallas kernels: 50.7 us -> 51.6 us  [on_device(): pl.pallas_call(functools.partial(gather_kernel, loop, line, group, halves...]
where the time goes in v2:
time: 58.8 us; the launch traced here: 58.7 us
  Pallas kernels  57 us (97%)
  local copies, waits for them, and re-layouts  1.6 us (3%)
    pallas_call x1, Pallas kernels, on_device(): pl.pallas_call(functools.partial(gather_kernel, loop, line, group, halves...  51.6 us
    pallas_call x1, Pallas kernels, on_device(): pl.pallas_call(functools.partial(lag_kernel, 1.0 / (F * seg_count)), out_...  5.44 us
    unnamed x8, local copies, waits for them, and re-layouts  1.6 us

profile of v2, /device:TPU:0, one launch (start us, length us, event | category | flops | bytes accessed | tf_op | source)
XLA Modules:
  0.0 58.7 jit_solution(16137833795439804230)
XLA Ops:
  0.0 0.0 copy-start.1
  0.0 0.0 copy-start.2
  0.0 0.0 copy-start.3
  0.0 51.6 %gather_products.1 = bf16[2,4,2,2,256,128]{5,4,3,2,1,0:T(8,128)(2,1)} custom-call(s32[1,2,2]{2,1,0:T(2,128)} %pairs_hbm.1, s32[1,2]{1,0:T(1,128)} %offsets_hbm.1, f32[4,512,256]{2,1,0:T(8,128)} %phases_hbm.1), custom_call_target="tpu_custom_call" | custom-call | tf_op jit(solution)/shard_map/gather_products/pallas_call | solution.py:350
  51.6 0.0 copy-done.1
  51.6 0.0 copy-done.2
  51.6 0.0 copy-done.3
  51.7 0.0 copy-start
  51.7 1.6 %copy-done = bf16[2,4,2,2,256,128]{5,4,3,2,1,0:T(8,128)(2,1)S(1)} copy-done((bf16[2,4,2,2,256,128]{5,4,3,2,1,0:T(8,128)(2,1)S(1)}, bf16[2,4,2,2,256,128]{5,4,3,2,1,0:T(8,128)(2,1)}, u32[]{:S(2)}) %copy-start) | copy-done | bytes 2097176
  53.2 5.4 %lag_sums.1 = f32[2,32,16384]{2,1,0:T(8,128)} custom-call(s32[2]{0:T(128)S(1)} %bitcast.6, s32[2]{0:T(128)S(1)} %bitcast.5, s32[1]{0:T(128)} %bitcast.2.place_ref, bf16[256,256]{1,0:T(8,128)(2,1)S(1)} %copy-done.1, bf16[2,8,512,128]{3,2,1,0:T(8,128)(2,1)S(1)} %bitcast.4), custom_call_target="tpu_custom_call" | custom-call | tf_op jit(solution)/shard_map/lag_sums/pallas_call | solution.py:390
Async XLA Ops:
  0.0 51.6 %copy-start.1 = (bf16[256,256]{1,0:T(8,128)(2,1)S(1)}, bf16[256,256]{1,0:T(8,128)(2,1)}, u32[]{:S(2)}) copy-start(bf16[256,256]{1,0:T(8,128)(2,1)} %constant.6.clone.table_ref) | copy-start | bytes 393220
  0.0 51.6 %copy-start.2 = (s32[1,2]{1,0:T(1,128)S(1)}, s32[1,2]{1,0:T(1,128)}, u32[]{:S(2)}) copy-start(s32[1,2]{1,0:T(1,128)} %offsets_hbm.1) | copy-start | bytes 28
  0.0 51.6 %copy-start.3 = (s32[1,2,1]{1,2,0:T(1,128)S(1)}, s32[1,2,1]{1,2,0:T(1,128)}, u32[]{:S(2)}) copy-start(s32[1,2,1]{1,2,0:T(1,128)} %param.8) | copy-start | bytes 28
  51.7 1.6 %copy-start = (bf16[2,4,2,2,256,128]{5,4,3,2,1,0:T(8,128)(2,1)S(1)}, bf16[2,4,2,2,256,128]{5,4,3,2,1,0:T(8,128)(2,1)}, u32[]{:S(2)}) copy-start(bf16[2,4,2,2,256,128]{5,4,3,2,1,0:T(8,128)(2,1)} %gather_products.1) | copy-start | bytes 6291460

commit v3 on v2

--- a/solution.py
+++ b/solution.py
@@ -16,6 +16,7 @@
 LAGS = 32
 ROW_STEP = 32
 SUBLANES = 16
+ABREAST = 4
 MESH = pl.DeviceIdType.MESH
 
 SIN_TERMS = (
@@ -164,34 +165,47 @@
         return chosen
 
     tile_copies = {}
-    asked_tiles = []
-    for g in range(freq_local // group):
-        for f in range(g * group, (g + 1) * group):
-            fetched[2 + f].wait()
-
-            @pl.loop(0, block_width // ROW_STEP)
-            def _(step):
-                rows = pl.ds(pl.multiple_of(step * ROW_STEP, ROW_STEP), ROW_STEP)
-                c, s = cos_sin(phases_ref[f, rows, :])
-                spec[f, rows, 0:seg_count] = c.astype(jnp.bfloat16)
-                spec[f, rows, seg_count:] = s.astype(jnp.bfloat16)
-
-        for o in range(steps):
-            if g == 0:
-                want_copies[o].wait_recv()
-                asked_tiles.append(jnp.max(asked[o]))
+    asked_tiles = {}
+
+    def make_spectra(f):
+        fetched[2 + f].wait()
+
+        @pl.loop(0, block_width // ROW_STEP)
+        def _(step):
+            rows = pl.ds(pl.multiple_of(step * ROW_STEP, ROW_STEP), ROW_STEP)
+            c, s = cos_sin(phases_ref[f, rows, :])
+            spec[f, rows, 0:seg_count] = c.astype(jnp.bfloat16)
+            spec[f, rows, seg_count:] = s.astype(jnp.bfloat16)
+
+    def send_tile(o, f):
+        if o not in asked_tiles:
+            want_copies[o].wait_recv()
+            asked_tiles[o] = jnp.max(asked[o])
+        going[o, f] = tile_of(f, asked_tiles[o])
+        copy = pltpu.make_async_remote_copy(
+            src_ref=going.at[o, f],
+            dst_ref=coming.at[o, f],
+            send_sem=tile_send.at[o, f],
+            recv_sem=tile_recv.at[o, f],
+            device_id=at_chan(-(o + 1)),
+            device_id_type=MESH,
+        )
+        copy.start()
+        tile_copies[o, f] = copy
+
+    pieces = [(o, g) for g in range(freq_local // group) for o in range(steps)]
+
+    def send_piece(number):
+        if number < len(pieces):
+            o, g = pieces[number]
             for f in range(g * group, (g + 1) * group):
-                going[o, f] = tile_of(f, asked_tiles[o])
-                copy = pltpu.make_async_remote_copy(
-                    src_ref=going.at[o, f],
-                    dst_ref=coming.at[o, f],
-                    send_sem=tile_send.at[o, f],
-                    recv_sem=tile_recv.at[o, f],
-                    device_id=at_chan(-(o + 1)),
-                    device_id_type=MESH,
-                )
-                copy.start()
-                tile_copies[o, f] = copy
+                send_tile(o, f)
+
+    for f in range(group):
+        make_spectra(f)
+        send_tile(0, f)
+    for f in range(group, freq_local):
+        make_spectra(f)
 
     units = [
         (o, g, h)
@@ -242,8 +256,10 @@
             o, g, h = units[turn]
             if h == 0:
                 for n in range(group):
+                    tile_copies[o, g * group + n].wait_recv()
+                send_piece(turn // halves + 1)
+                for n in range(group):
                     f = g * group + n
-                    tile_copies[o, f].wait_recv()
                     left = tile_of(f, left_tiles[o])
                     swapped = jnp.concatenate(
                         [left[:, seg_count:], -left[:, :seg_count]], axis=1
@@ -320,11 +336,11 @@
             [cross_ref[0, u, start : start + SUBLANES, :] for u in range(groups)], axis=0
         )
 
-    for at in range(0, block_rows // SUBLANES, 2):
-        pair = jnp.concatenate([stacked(at), stacked(at + 1)], axis=1)
+    for at in range(0, block_rows // SUBLANES, ABREAST):
+        beside = jnp.concatenate([stacked(at + n) for n in range(ABREAST)], axis=1)
         lagged = jnp.dot(
             table,
-            jnp.concatenate([pair, pair], axis=0),
+            jnp.concatenate([beside, beside], axis=0),
             preferred_element_type=jnp.float32,
         )
         for i in range(rows_at_once):
@@ -332,7 +348,7 @@
             real = lagged[start : start + LAGS]
             imag = lagged[start + LAGS : start + 2 * LAGS]
             envelope = (real * real + imag * imag) * scale
-            for n in range(2):
+            for n in range(ABREAST):
                 place = ((at + n) * rows_at_once + i) * width
                 out_ref[0, :, place : place + width] = envelope[:, n * width : (n + 1) * width]
 
@@ -401,7 +417,7 @@
                 (1, LAGS, rows * TILE), lambda slot, part, *_: (slot, 0, part)
             ),
         ),
-        compiler_params=pltpu.CompilerParams(vmem_limit_bytes=24 * 2**20),
+        compiler_params=pltpu.CompilerParams(vmem_limit_bytes=58 * 2**20),
         name="lag_sums",
     )(
         owners.reshape(list_len),

time: 58.8 us -> 56.7 us (0.964)
  local copies, waits for them, and re-layouts: 1.6 us -> 0 us
  Pallas kernels: 57 us -> 56.4 us
    pallas_call x1, Pallas kernels: 51.6 us -> 48.6 us  [on_device(): pl.pallas_call(functools.partial(gather_kernel, loop, line, group, halves...]
    pallas_call x1, Pallas kernels: 5.44 us -> 7.81 us  [on_device(): pl.pallas_call(functools.partial(lag_kernel, 1.0 / (F * seg_count)), out_...]
    unnamed x8 -> x0, local copies, waits for them, and re-layouts: 1.6 us -> none
where the time goes in v3:
time: 56.7 us; the launch traced here: 56.4 us
  Pallas kernels  56.4 us (99%)
    pallas_call x1, Pallas kernels, on_device(): pl.pallas_call(functools.partial(gather_kernel, loop, line, group, halves...  48.6 us
    pallas_call x1, Pallas kernels, on_device(): pl.pallas_call(functools.partial(lag_kernel, 1.0 / (F * seg_count)), out_...  7.81 us

profile of v3, /device:TPU:0, one launch (start us, length us, event | category | flops | bytes accessed | tf_op | source)
XLA Modules:
  0.0 56.4 jit_solution(12855498587128679961)
XLA Ops:
  0.0 48.6 %gather_products.1 = bf16[2,4,2,2,256,128]{5,4,3,2,1,0:T(8,128)(2,1)} custom-call(s32[1,2,2]{2,1,0:T(2,128)} %pairs_hbm.1, s32[1,2]{1,0:T(1,128)} %offsets_hbm.1, f32[4,512,256]{2,1,0:T(8,128)} %phases_hbm.1), custom_call_target="tpu_custom_call" | custom-call | tf_op jit(solution)/shard_map/gather_products/pallas_call | solution.py:366
  48.6 7.8 %lag_sums.1 = f32[2,32,16384]{2,1,0:T(8,128)} custom-call(s32[2]{0:T(128)} %bitcast.6, s32[2]{0:T(128)} %bitcast.5, s32[1]{0:T(128)} %bitcast.2.place_ref, bf16[256,256]{1,0:T(8,128)(2,1)} %constant.6.clone.table_ref, bf16[2,8,512,128]{3,2,1,0:T(8,128)(2,1)} %bitcast.4), custom_call_target="tpu_custom_call" | custom-call | tf_op jit(solution)/shard_map/lag_sums/pallas_call | solution.py:406

commit v4 on v3

--- a/solution.py
+++ b/solution.py
@@ -16,7 +16,7 @@
 LAGS = 32
 ROW_STEP = 32
 SUBLANES = 16
-ABREAST = 4
+ABREAST = 2
 MESH = pl.DeviceIdType.MESH
 
 SIN_TERMS = (
@@ -396,7 +396,7 @@
         name="gather_products",
     )(tile_pairs, block_offsets, phases)
 
-    rows = 32
+    rows = 128
     table = row_table(2 * group, SUBLANES // (2 * group))
     place = lax.axis_index("freq").astype(jnp.int32).reshape(1)
 

time: 56.7 us -> 53.6 us (0.945)
  Pallas kernels: 56.4 us -> 53.4 us
    pallas_call x1, Pallas kernels: 7.81 us -> 4.79 us  [on_device(): pl.pallas_call(functools.partial(lag_kernel, 1.0 / (F * seg_count)), out_...]
where the time goes in v4:
time: 53.6 us; the launch traced here: 53.4 us
  Pallas kernels  53.4 us (100%)
    pallas_call x1, Pallas kernels, on_device(): pl.pallas_call(functools.partial(gather_kernel, loop, line, group, halves...  48.6 us
    pallas_call x1, Pallas kernels, on_device(): pl.pallas_call(functools.partial(lag_kernel, 1.0 / (F * seg_count)), out_...  4.79 us

profile of v4, /device:TPU:0, one launch (start us, length us, event | category | flops | bytes accessed | tf_op | source)
XLA Modules:
  0.0 53.4 jit_solution(4620276023497872356)
XLA Ops:
  0.0 48.6 %gather_products.1 = bf16[2,4,2,2,256,128]{5,4,3,2,1,0:T(8,128)(2,1)} custom-call(s32[1,2,2]{2,1,0:T(2,128)} %pairs_hbm.1, s32[1,2]{1,0:T(1,128)} %offsets_hbm.1, f32[4,512,256]{2,1,0:T(8,128)} %phases_hbm.1), custom_call_target="tpu_custom_call" | custom-call | tf_op jit(solution)/shard_map/gather_products/pallas_call | solution.py:366
  48.6 4.8 %lag_sums.1 = f32[2,32,16384]{2,1,0:T(8,128)} custom-call(s32[2]{0:T(128)} %bitcast.6, s32[2]{0:T(128)} %bitcast.5, s32[1]{0:T(128)} %bitcast.2.place_ref, bf16[256,256]{1,0:T(8,128)(2,1)} %constant.6.clone.table_ref, bf16[2,8,512,128]{3,2,1,0:T(8,128)(2,1)} %bitcast.4), custom_call_target="tpu_custom_call" | custom-call | tf_op jit(solution)/shard_map/lag_sums/pallas_call | solution.py:406
